TPU v7x, 256 devices: a whole 4x4x8 slice. The times are simulated.
256 devices in a mesh: row: 8 (over x, core), col: 2 (over z_lo), chan: 16 (over y, z_hi).
Axes of the slice: x: 4, y: 4, z: 8 (z_hi: 4, z_lo: 2; z = z_hi * 2 + z_lo), core: 2. Of those that a mesh axis runs over, the one named last changes fastest.
Arguments:
- pair: float32 [128, 1024, 1024], P('chan', 'row', 'col'), may hold values from -6 to 6
- pair_mask: int32 [1024, 1024], P('row', 'col'), may hold values 0 or 1
- norm_gain: float32 [128], replicated, may hold values from 0.1 to 1.9
- norm_bias: float32 [128], replicated, may hold values from -3 to 3
- in_weight: bfloat16 [128, 512], replicated, may hold values from -0.5 to 0.5
- gate_weight: bfloat16 [128, 128], replicated, may hold values from -0.5 to 0.5
- hidden_gain: float32 [128], replicated, may hold values from 0.1 to 1.9
- hidden_bias: float32 [128], replicated, may hold values from -3 to 3
- out_weight: bfloat16 [128, 128], replicated, may hold values from -0.5 to 0.5
Outputs:
- update: float32 [128, 1024, 1024], P('chan', 'row', 'col')
All inputs are finite; a program needn't handle non-finite values. No bound on the sum of `pair_mask` on one device may be relied on, other than what follows from the above.
Results may differ from a plain program's by a relative error of at most 0.0031.
Values may be sent and summed in bfloat16 or wider, within the bound.
A program may use at most 64 MiB of HBM per device.

v0:
```python
import jax
import jax.numpy as jnp
from jax import lax
from jax.sharding import PartitionSpec as P

EPS = 1e-05


def flat_norm(values, gain, bias):
    mean = jnp.mean(values, axis=0, keepdims=True)
    centred = values - mean
    var = jnp.mean(centred * centred, axis=0, keepdims=True)
    return centred * lax.rsqrt(var + EPS) * gain[:, None] + bias[:, None]


def shards(
    pair,
    pair_mask,
    norm_gain,
    norm_bias,
    in_weight,
    gate_weight,
    hidden_gain,
    hidden_bias,
    out_weight,
):
    groups = lax.axis_size("chan")
    local_rows = pair.shape[1]
    local_cols = pair.shape[2]
    flat_pairs = local_rows * local_cols
    width = flat_pairs // groups
    hidden_width = out_weight.shape[0]
    flat_pair = pair.reshape(pair.shape[0], flat_pairs)
    grouped = lax.all_to_all(flat_pair, "chan", split_axis=1, concat_axis=0, tiled=True)
    offset = lax.axis_index("chan") * width
    mask_part = lax.dynamic_slice_in_dim(pair_mask.reshape(flat_pairs), offset, width, 0).astype(
        jnp.float32
    )
    normed = flat_norm(grouped, norm_gain, norm_bias).astype(jnp.bfloat16)
    proj = jnp.einsum("cp,cf->fp", normed, in_weight, preferred_element_type=jnp.float32)
    left = (
        jax.nn.sigmoid(proj[:hidden_width]) * proj[hidden_width : 2 * hidden_width] * mask_part
    ).astype(jnp.bfloat16)
    right = (
        jax.nn.sigmoid(proj[2 * hidden_width : 3 * hidden_width])
        * proj[3 * hidden_width :]
        * mask_part
    ).astype(jnp.bfloat16)
    gate = jax.nn.sigmoid(
        jnp.einsum("ep,ec->cp", normed, gate_weight, preferred_element_type=jnp.float32)
    )
    left_flat, right_flat = (
        lax.all_to_all(left, "chan", split_axis=0, concat_axis=1, tiled=True),
        lax.all_to_all(right, "chan", split_axis=0, concat_axis=1, tiled=True),
    )
    left_cols = left_flat.reshape(left_flat.shape[0], local_rows, local_cols)
    right_cols = right_flat.reshape(right_flat.shape[0], local_rows, local_cols)
    partial_sums = jnp.einsum(
        "hik,hjk->hij",
        left_cols,
        lax.all_gather(right_cols, "row", axis=1, tiled=True),
        preferred_element_type=jnp.float32,
    )
    summed = lax.psum_scatter(partial_sums, "col", scatter_dimension=2, tiled=True)
    hidden = lax.all_to_all(
        summed.reshape(summed.shape[0], flat_pairs), "chan", split_axis=1, concat_axis=0, tiled=True
    )
    hnorm = flat_norm(hidden, hidden_gain, hidden_bias).astype(jnp.bfloat16)
    projected = jnp.einsum("hp,hc->cp", hnorm, out_weight, preferred_element_type=jnp.float32)
    update = gate * projected
    owned = lax.all_to_all(update, "chan", split_axis=0, concat_axis=1, tiled=True)
    return owned.reshape(owned.shape[0], local_rows, local_cols)


def solution(mesh):
    placed = (P("chan", "row", "col"), P("row", "col"), P(), P(), P(), P(), P(), P(), P())
    return jax.shard_map(
        shards, mesh=mesh, in_specs=placed, out_specs=P("chan", "row", "col"), check_vma=False
    )
```

profile of v0, /device:TPU:35, one launch (start us, length us, event | category | flops | bytes accessed | tf_op | source)
XLA Modules:
  0.0 368.3 jit_solution(5541714682189594698)
XLA Ops:
  6.5 0.0 copy-start
  6.5 1.8 all_to_all.64
  8.3 2.5 copy.22
  10.9 0.0 copy-start.2
  10.9 10.2 %all-to-all-start = ((f32[8,16,4096]{2,0,1:T(8,128)}), f32[8,16,4096]{2,0,1:T(8,128)S(1)}, u32[]{:S(2)}, u32[]{:S(2)}) async-start(f32[8,16,4096]{2,0,1:T(8,128)} %copy.22), calls=%async_computation | async-start | bytes 4194304 | tf_op jit(solution)/shard_map/all_to_all | solution.py:34
  21.0 0.0 all-gather.2.cloned.1.call-start
  21.1 0.0 copy-done.2
  21.1 0.1 copy.27
  21.2 0.0 copy-start.4
  21.2 0.0 copy-start.5
  21.2 49.0 %all-to-all-done = f32[8,16,4096]{2,0,1:T(8,128)S(1)} async-done(((f32[8,16,4096]{2,0,1:T(8,128)}), f32[8,16,4096]{2,0,1:T(8,128)S(1)}, u32[]{:S(2)}, u32[]{:S(2)}) %all-to-all-start) | async-done | bytes 2097184 | tf_op jit(solution)/shard_map/all_to_all | solution.py:34
  70.2 0.1 reduce_sum.36
  70.3 0.2 fusion.25
  70.6 0.0 copy-done
  70.6 0.0 copy-done.4
  70.6 0.0 copy-done.5
  70.6 1.4 convolution_bitcast_fusion
  72.0 1.1 fusion.32
  73.1 35.2 %all_to_all.86 = bf16[16,8,4096]{2,1,0:T(8,128)(2,1)S(1)} all-to-all(bf16[16,8,4096]{2,1,0:T(8,128)(2,1)S(1)} %get-tuple-element.5), channel_id=1, replica_groups=mesh['row'=8,'col'=2,'chan'=16] {'chan'}, dimensions={0} | all-to-all | bytes 2097152 | tf_op jit(solution)/shard_map/all_to_all | solution.py:54
  108.2 1.6 copy.24
  109.8 2.4 reshape.75
  112.2 0.0 all-gather.2.cloned.1.call-update
  112.2 0.0 reduce-scatter.2.cloned.1.call-start
  112.2 31.3 %all_to_all.87 = bf16[16,8,4096]{2,1,0:T(8,128)(2,1)S(1)} all-to-all(bf16[16,8,4096]{2,1,0:T(8,128)(2,1)S(1)} %get-tuple-element.6), channel_id=1, replica_groups=mesh['row'=8,'col'=2,'chan'=16] {'chan'}, dimensions={0} | all-to-all | bytes 2097152 | tf_op jit(solution)/shard_map/all_to_all | solution.py:53
  143.6 0.6 copy.23
  144.1 1.3 reshape.74
  145.5 15.7 %all-gather.2.cloned.1.call-done = bf16[8,1024,512]{2,1,0:T(8,128)(2,1)} async-done(((bf16[8,128,512]{2,1,0:T(8,128)(2,1)}), bf16[8,1024,512]{2,1,0:T(8,128)(2,1)}) %all-gather.2.cloned.1.call-update) | async-done | bytes 8388624 | tf_op jit(solution)/shard_map/all_gather | solution.py:61
  161.2 8.5 %fusion.35 = f32[8,128,1024]{2,1,0:T(8,128)} fusion(bf16[8,128,512]{2,1,0:T(8,128)(2,1)} %reshape.74, bf16[8,1024,512]{2,1,0:T(8,128)(2,1)} %all-gather.2.cloned.1.call-done), kind=kOutput, calls=%fused_computation.48 | convolution fusion | flops 1073741824 | bytes 13631488 | tf_op jit(solution)/shard_map/hik,hjk->hij/dot_general | solution.py:58
  169.7 0.0 reduce-scatter.2.cloned.1.call-update
  169.7 59.1 %reduce-scatter.2.cloned.1.call-done = f32[8,128,512]{2,1,0:T(8,128)} async-done(((f32[8,128,1024]{2,1,0:T(8,128)}), f32[8,128,512]{2,1,0:T(8,128)}) %reduce-scatter.2.cloned.1.call-update) | async-done | bytes 2097168 | tf_op jit(solution)/shard_map/reduce_scatter | solution.py:64
  228.8 2.7 all_to_all.74
  231.5 4.1 %copy.25 = f32[8,16,4096]{2,0,1:T(8,128)} copy(f32[8,16,4096]{2,1,0:T(8,128)} %all_to_all.74) | data formatting | bytes 4194304 | tf_op jit(solution)/shard_map/all_to_all | solution.py:65
  235.6 0.0 copy-start.8
  235.6 9.5 %all-to-all-start.3 = ((f32[8,16,4096]{2,0,1:T(8,128)}), f32[8,16,4096]{2,0,1:T(8,128)}, u32[]{:S(2)}, u32[]{:S(2)}) async-start(f32[8,16,4096]{2,0,1:T(8,128)} %copy.25), calls=%async_computation.4 | async-start | bytes 4194304 | tf_op jit(solution)/shard_map/all_to_all | solution.py:65
  245.1 0.0 copy-done.8
  245.1 2.2 fusion.3
  247.4 47.8 %all-to-all-done.3 = f32[8,16,4096]{2,0,1:T(8,128)} async-done(((f32[8,16,4096]{2,0,1:T(8,128)}), f32[8,16,4096]{2,0,1:T(8,128)}, u32[]{:S(2)}, u32[]{:S(2)}) %all-to-all-start.3) | async-done | bytes 2097184 | tf_op jit(solution)/shard_map/all_to_all | solution.py:65
  295.1 1.7 reduce_sum.38
  296.8 0.0 copy-start.1
  296.9 2.0 fusion.23
  298.9 0.0 copy-done.3
  298.9 0.0 copy-done.6
  298.9 0.0 copy-done.7
  298.9 0.2 copy-done.1
  299.1 2.3 fusion
  301.3 57.4 %all_to_all.88 = f32[16,8,4096]{2,1,0:T(8,128)S(1)} all-to-all(f32[16,8,4096]{2,1,0:T(8,128)S(1)} %fusion), channel_id=1, replica_groups=mesh['row'=8,'col'=2,'chan'=16] {'chan'}, dimensions={0} | all-to-all | bytes 4194304 | tf_op jit(solution)/shard_map/all_to_all | solution.py:71
  358.7 1.2 copy.26
  359.9 1.5 reshape.76
  (8 shorter events, 0.0 us)
Async XLA Ops:
  6.5 64.0 %copy-start = (bf16[128,512]{1,0:T(8,128)(2,1)S(1)}, bf16[128,512]{1,0:T(8,128)(2,1)}, u32[]{:S(2)}) copy-start(bf16[128,512]{1,0:T(8,128)(2,1)} %param.13) | copy-start | bytes 393220
  10.9 10.2 %copy-start.2 = (s32[128,512]{1,0:T(8,128)S(1)}, s32[128,512]{1,0:T(8,128)}, u32[]{:S(2)}) copy-start(s32[128,512]{1,0:T(8,128)} %param.10) | copy-start | bytes 786436
  10.9 59.3 %all-to-all-start = ((f32[8,16,4096]{2,0,1:T(8,128)}), f32[8,16,4096]{2,0,1:T(8,128)S(1)}, u32[]{:S(2)}, u32[]{:S(2)}) async-start(f32[8,16,4096]{2,0,1:T(8,128)} %copy.22), calls=%async_computation | async-start | bytes 4194304 | tf_op jit(solution)/shard_map/all_to_all | solution.py:34
  21.0 140.2 %all-gather.2.cloned.1.call-start = ((), (), s32[]{:S(2)}) async-start(), calls=%async_computation.6 | async-start | bytes 9437184 | tf_op jit(solution)/shard_map/all_gather | solution.py:61
  21.2 49.4 %copy-start.4 = (f32[128]{0:T(128)S(1)}, f32[128]{0:T(128)}, u32[]{:S(2)}) copy-start(f32[128]{0:T(128)} %param.12) | copy-start | bytes 1540
  21.2 49.4 %copy-start.5 = (f32[128]{0:T(128)S(1)}, f32[128]{0:T(128)}, u32[]{:S(2)}) copy-start(f32[128]{0:T(128)} %param.11) | copy-start | bytes 1540
  112.2 116.6 %reduce-scatter.2.cloned.1.call-start = ((), (), s32[]{:S(2)}) async-start(), calls=%async_computation.7 | async-start | bytes 6291456 | tf_op jit(solution)/shard_map/reduce_scatter | solution.py:64
  235.6 9.5 %copy-start.8 = (bf16[128,128]{1,0:T(8,128)(2,1)S(1)}, bf16[128,128]{1,0:T(8,128)(2,1)}, u32[]{:S(2)}) copy-start(bf16[128,128]{1,0:T(8,128)(2,1)} %param.14) | copy-start | bytes 98308
  235.6 59.5 %all-to-all-start.3 = ((f32[8,16,4096]{2,0,1:T(8,128)}), f32[8,16,4096]{2,0,1:T(8,128)}, u32[]{:S(2)}, u32[]{:S(2)}) async-start(f32[8,16,4096]{2,0,1:T(8,128)} %copy.25), calls=%async_computation.4 | async-start | bytes 4194304 | tf_op jit(solution)/shard_map/all_to_all | solution.py:65
  247.4 51.5 %copy-start.3 = (bf16[128,128]{1,0:T(8,128)(2,1)S(1)}, bf16[128,128]{1,0:T(8,128)(2,1)}, u32[]{:S(2)}) copy-start(bf16[128,128]{1,0:T(8,128)(2,1)} %param.17) | copy-start | bytes 98308
  247.4 51.5 %copy-start.6 = (f32[128]{0:T(128)S(1)}, f32[128]{0:T(128)}, u32[]{:S(2)}) copy-start(f32[128]{0:T(128)} %param.16) | copy-start | bytes 1540
  247.4 51.5 %copy-start.7 = (f32[128]{0:T(128)S(1)}, f32[128]{0:T(128)}, u32[]{:S(2)}) copy-start(f32[128]{0:T(128)} %param.15) | copy-start | bytes 1540
  296.8 2.2 copy-start.1
Sparse Core Ops, SparseCore 0:
  112.3 48.8 all-gather.1
  169.8 58.9 reduce-scatter.1
where the time goes:
time: 369 us; the launch traced here: 368 us
  waiting for transfers between devices  172 us (47%)
  blocking collectives  124 us (34%)
  local copies, waits for them, and re-layouts  20 us (5%)
  starting transfers between devices  19.7 us (5%)
  matrix products  14.3 us (4%)
  between operations  13.6 us (4%)
  other arithmetic  5.16 us (1%)
    reduce_scatter x1, waiting for transfers between devices, shards(): lax.psum_scatter(partial_sums, 'col', scatter_dimension=2, tiled=True)  59.1 us
    all_to_all x1, blocking collectives, shards(): lax.all_to_all(update, 'chan', split_axis=0, concat_axis=1, tiled=True)  57.4 us
    all_to_all x1, waiting for transfers between devices, shards(): lax.all_to_all(flat_pair, 'chan', split_axis=1, concat_axis=0, tiled=True)  49 us
    all_to_all x1, waiting for transfers between devices, shards(): lax.all_to_all(summed.reshape(summed.shape[0], flat_pairs), 'chan', split...  47.8 us
    all_to_all x1, blocking collectives, shards(): lax.all_to_all(right, 'chan', split_axis=0, concat_axis=1, tiled=True)  35.2 us
    all_to_all x1, blocking collectives, shards(): lax.all_to_all(left, 'chan', split_axis=0, concat_axis=1, tiled=True)  31.3 us
    all_gather x1, waiting for transfers between devices, shards(): lax.all_gather(right_cols, 'row', axis=1, tiled=True)  15.7 us
    all_to_all x1, starting transfers between devices, shards(): lax.all_to_all(flat_pair, 'chan', split_axis=1, concat_axis=0, tiled=True)  10.2 us
  transfers between devices with their start and end apart: 4, of which 4 were waited for; matrix products, arithmetic and copies ran while one was open for 1% of the time, Pallas kernels for 0%

commit v1 on v0

v1 whole, which is shorter than its diff:
```python
import jax
import jax.numpy as jnp
from jax import lax
from jax.sharding import PartitionSpec as P

EPS = 1e-05
AXES = ("row", "col", "chan")
STEP = 6.0 / 32767.0


def shards(
    pair,
    pair_mask,
    norm_gain,
    norm_bias,
    in_weight,
    gate_weight,
    hidden_gain,
    hidden_bias,
    out_weight,
):
    hid = 128
    chan = lax.axis_index("chan")
    row = lax.axis_index("row")
    fixed = jnp.round(pair * (1.0 / STEP)).astype(jnp.int16)
    blocks = fixed.reshape(8, 4, 32, 4, 128).transpose(1, 3, 0, 2, 4).reshape(16, 8, 32, 128)
    grouped = lax.all_to_all(blocks, "chan", split_axis=0, concat_axis=0, tiled=True)
    values = grouped.reshape(128, 4096).astype(jnp.float32) * STEP
    mask = lax.dynamic_slice(pair_mask, ((chan // 4) * 32, (chan % 4) * 128), (32, 128))
    mask = mask.reshape(4096).astype(jnp.float32)
    mean = jnp.mean(values, axis=0, keepdims=True)
    centred = values - mean
    var = jnp.mean(centred * centred, axis=0, keepdims=True)
    normed = centred * lax.rsqrt(var + EPS) * norm_gain[:, None] + norm_bias[:, None]
    normed = normed.astype(jnp.bfloat16)
    proj = jnp.einsum("cp,cf->fp", normed, in_weight, preferred_element_type=jnp.float32)
    left = (jax.nn.sigmoid(proj[:hid]) * proj[hid : 2 * hid] * mask).astype(jnp.bfloat16)
    right = (jax.nn.sigmoid(proj[2 * hid : 3 * hid]) * proj[3 * hid :] * mask).astype(jnp.bfloat16)
    both = jnp.stack([left.reshape(4, 32, 2, 16, 128), right.reshape(4, 32, 2, 16, 128)], axis=3)
    both = both.transpose(0, 2, 1, 3, 4, 5).reshape(256, 2, 16, 128)
    both = lax.all_to_all(both, AXES, split_axis=0, concat_axis=0, tiled=True)
    both = both.reshape(8, 2, 4, 4, 2, 16, 128).transpose(4, 0, 2, 5, 1, 3, 6).reshape(2, 512, 1024)
    own = both[1].reshape(32, 16, 1024)
    other = lax.ppermute(both[1], "row", [(r, r ^ 1) for r in range(8)]).reshape(32, 16, 1024)
    odd = row % 2 == 1
    full = jnp.stack([jnp.where(odd, other, own), jnp.where(odd, own, other)], axis=1)
    full = full.reshape(1024, 1024)
    hidden = jnp.einsum("ik,jk->ij", both[0], full, preferred_element_type=jnp.float32)
    hidden = hidden.astype(jnp.bfloat16)
    hidden = hidden.reshape(8, 4, 16, 2, 4, 128).transpose(0, 3, 1, 4, 2, 5).reshape(256, 16, 128)
    hidden = lax.all_to_all(hidden, AXES, split_axis=0, concat_axis=0, tiled=True)
    hidden = hidden.reshape(4, 2, 32, 16, 128).transpose(0, 2, 1, 3, 4).reshape(128, 4096)
    wide = hidden.astype(jnp.float32)
    nu = jnp.mean(wide, axis=0, keepdims=True)
    dev = wide - nu
    tau = jnp.mean(dev * dev, axis=0, keepdims=True)
    scaled = hidden_gain[:, None] * out_weight.astype(jnp.float32)
    high = lax.reduce_precision(scaled, 8, 7)
    low = lax.reduce_precision(scaled - high, 8, 7)
    pieces = jnp.concatenate([high, low], axis=0).astype(jnp.bfloat16)
    raw = jnp.einsum(
        "hp,hc->cp",
        jnp.concatenate([hidden, hidden], axis=0),
        pieces,
        preferred_element_type=jnp.float32,
    )
    column = jnp.sum(high + low, axis=0)
    offset = jnp.sum(hidden_bias[:, None] * out_weight.astype(jnp.float32), axis=0)
    projected = (raw - nu * column[:, None]) * lax.rsqrt(tau + EPS) + offset[:, None]
    gate = jax.nn.sigmoid(
        jnp.einsum("ep,ec->cp", normed, gate_weight, preferred_element_type=jnp.float32)
    )
    update = (gate * projected).astype(jnp.bfloat16).reshape(16, 8, 32, 128)
    owned = lax.all_to_all(update, "chan", split_axis=0, concat_axis=0, tiled=True)
    owned = owned.reshape(4, 4, 8, 32, 128).transpose(2, 0, 3, 1, 4).reshape(8, 128, 512)
    return owned.astype(jnp.float32)


def solution(mesh):
    placed = (P("chan", "row", "col"), P("row", "col"), P(), P(), P(), P(), P(), P(), P())
    return jax.shard_map(
        shards, mesh=mesh, in_specs=placed, out_specs=P("chan", "row", "col"), check_vma=False
    )
```

time: 369 us -> 216 us (0.59)
  the two profiles are of different devices: /device:TPU:35 before, /device:TPU:1 now
where the time goes in v1:
time: 216 us; the launch traced here: 215 us
  blocking collectives  95.7 us (44%)
  waiting for transfers between devices  53.3 us (25%)
  local copies, waits for them, and re-layouts  28.8 us (13%)
  starting transfers between devices  19.2 us (9%)
  matrix products  9.32 us (4%)
  other arithmetic  8.38 us (4%)
    all_to_all x1, blocking collectives, shards(): both = lax.all_to_all(both, AXES, split_axis=0, concat_axis=0, tiled=True)  63.4 us
    all_to_all x1, blocking collectives, shards(): lax.all_to_all(update, 'chan', split_axis=0, concat_axis=0, tiled=True)  32.3 us
    all_to_all x1, waiting for transfers between devices, shards(): lax.all_to_all(hidden, AXES, split_axis=0, concat_axis=0, tiled=True)  28 us
    all_to_all x1, waiting for transfers between devices, shards(): lax.all_to_all(blocks, 'chan', split_axis=0, concat_axis=0, tiled=True)  25.3 us
    all_to_all x1, starting transfers between devices, shards(): lax.all_to_all(blocks, 'chan', split_axis=0, concat_axis=0, tiled=True)  11.7 us
    all_to_all x1, starting transfers between devices, shards(): lax.all_to_all(hidden, AXES, split_axis=0, concat_axis=0, tiled=True)  6.62 us
    unnamed x25, local copies, waits for them, and re-layouts  6.2 us
  transfers between devices with their start and end apart: 3, of which 2 were waited for; matrix products, arithmetic and copies ran while one was open for 4% of the time, Pallas kernels for 0%

profile of v1, /device:TPU:1, one launch (start us, length us, event | category | flops | bytes accessed | tf_op | source)
XLA Modules:
  0.0 215.0 jit_solution(9480763576614256171)
XLA Ops:
  0.0 2.0 round-nearest-even_convert_fusion
  2.0 0.3 reshape.160
  2.3 1.2 copy.21
  3.5 11.7 %all-to-all-start = ((s16[16,8,32,128]{3,2,1,0:T(8,128)(2,1)}), s16[16,8,32,128]{3,2,1,0:T(8,128)(2,1)S(1)}, u32[]{:S(2)}, u32[]{:S(2)}) async-start(s16[16,8,32,128]{3,2,1,0:T(8,128)(2,1)} %bitcast.1), calls=%async_computation | async-start | bytes 2097152 | tf_op jit(solution)/shard_map/all_to_all | solution.py:27
  15.3 0.7 convert_bitcast_fusion.1
  16.0 25.3 %all-to-all-done = s16[16,8,32,128]{3,2,1,0:T(8,128)(2,1)S(1)} async-done(((s16[16,8,32,128]{3,2,1,0:T(8,128)(2,1)}), s16[16,8,32,128]{3,2,1,0:T(8,128)(2,1)S(1)}, u32[]{:S(2)}, u32[]{:S(2)}) %all-to-all-start) | async-done | bytes 1048608 | tf_op jit(solution)/shard_map/all_to_all | solution.py:27
  41.3 0.4 fusion.27
  41.7 0.5 multiply_reduce_fusion
  42.3 2.1 convolution_bitcast_fusion
  44.4 2.0 fusion.20
  46.4 2.3 %copy.23 = bf16[128,4096]{1,0:T(8,128)(2,1)} copy(bf16[128,4096]{0,1:T(8,128)(2,1)} %get-tuple-element.8) | data formatting | bytes 2097152 | tf_op jit(solution)/shard_map/convert_element_type | solution.py:38
  48.7 2.4 %copy.35 = bf16[16,8,32,128]{3,2,1,0:T(8,128)(2,1)} copy(bf16[16,8,32,128]{3,1,2,0:T(8,128)(2,1)} %bitcast.81) | data formatting | bytes 2097152
  51.1 1.3 copy.22
  52.4 1.5 copy.34
  54.0 0.2 maximum_bitcast_fusion
  54.2 0.4 copy.24
  54.5 63.4 %all_to_all.20 = bf16[256,2,16,128]{3,2,1,0:T(8,128)(2,1)S(1)} all-to-all(bf16[256,2,16,128]{3,2,1,0:T(8,128)(2,1)S(1)} %bitcast.76), channel_id=1, replica_groups=mesh['row'=8,'col'=2,'chan'=16] {'row','col','chan'}, dimensions={0} | all-to-all | bytes 4194304 | tf_op jit(solution)/shard_map/all_to_all | solution.py:41
  118.0 1.1 copy.47
  119.0 2.2 %fusion.40 = (bf16[1,8,4,16,2,4,128]{6,5,4,3,2,1,0:T(4,128)(2,1)S(1)}, bf16[1,8,4,16,2,4,128]{6,5,4,3,2,1,0:T(4,128)(2,1)}) fusion(bf16[2,8,4,16,2,4,128]{6,5,4,3,2,1,0:T(4,128)(2,1)S(1)} %bitcast.75), kind=kLoop, calls=%fused_computation.70 | loop fusion | bytes 4194304 | tf_op jit(solution)/shard_map/slice | solution.py:44
  121.2 1.5 squeeze.7
  122.7 0.8 collective-permute-start
  123.5 1.5 reshape_squeeze.3
  125.1 2.6 %squeeze.6 = bf16[512,1024]{1,0:T(8,128)(2,1)} reshape(bf16[1,8,4,16,2,4,128]{6,5,4,3,2,1,0:T(4,128)(2,1)} %get-tuple-element.12) | data formatting | bytes 2097152 | tf_op jit(solution)/shard_map/squeeze | solution.py:48
  127.7 1.4 broadcast_select_fusion.1
  129.1 0.2 pad_maximum_fusion
  129.3 0.3 copy.26
  129.6 0.9 copy-done.3
  130.5 2.3 %convolution_convert_fusion = bf16[512,1024]{1,0:T(8,128)(2,1)} fusion(bf16[512,1024]{1,0:T(8,128)(2,1)S(1)} %copy-done.3, bf16[1024,1024]{1,0:T(8,128)(2,1)S(1)} %bitcast.86), kind=kOutput, calls=%fused_computation.46 | convolution fusion | flops 1074266112 | bytes 4194304 | tf_op jit(solution)/shard_map/ik,jk->ij/dot_general | solution.py:48
  132.8 1.8 reshape.166
  134.6 0.0 copy-start.4
  134.6 0.0 copy-start.9
  134.6 1.3 copy.27
  135.9 6.6 %all-to-all-start.2 = ((bf16[256,16,128]{2,1,0:T(8,128)(2,1)}), bf16[256,16,128]{2,1,0:T(8,128)(2,1)S(1)}, u32[]{:S(2)}, u32[]{:S(2)}) async-start(bf16[256,16,128]{2,1,0:T(8,128)(2,1)} %bitcast.79), calls=%async_computation.2 | async-start | bytes 2097152 | tf_op jit(solution)/shard_map/all_to_all | solution.py:51
  142.6 0.1 fusion.32
  142.7 2.9 %fusion.6 = f32[128,4096]{0,1:T(8,128)} fusion(bf16[128,128]{1,0:T(8,128)(2,1)S(1)} %copy-done.9, f32[16,8,32,128]{3,2,1,0:T(8,128)S(1)} %get-tuple-element.14, f32[128]{0:T(128)S(1)} %copy-done.5, f32[128]{0:T(128)S(1)} %copy-done.6, f32[4096]{0:T(1024)S(1)} %rsqrt_bitcast_fusion, f32[4096]{0:T(1024)S(1)} %get-tuple-element.17), kind=kOutput, calls=%fused_computation.9 | convolution fusion | flops 138412032 | bytes 4260864 | tf_op jit(solution)/shard_map/ep,ec->cp/dot_general | solution.py:71
  145.6 28.0 %all-to-all-done.2 = bf16[256,16,128]{2,1,0:T(8,128)(2,1)S(1)} async-done(((bf16[256,16,128]{2,1,0:T(8,128)(2,1)}), bf16[256,16,128]{2,1,0:T(8,128)(2,1)S(1)}, u32[]{:S(2)}, u32[]{:S(2)}) %all-to-all-start.2) | async-done | bytes 1048608 | tf_op jit(solution)/shard_map/all_to_all | solution.py:51
  173.6 0.2 copy_bitcast_fusion.2
  173.8 0.5 reshape.169
  174.3 0.2 convert_reduce_fusion
  174.5 0.3 fusion.9
  174.9 1.0 copy-done.10
  175.9 2.0 fusion.7
  177.9 0.5 copy.30
  178.5 0.2 copy.48
  178.7 32.3 %all_to_all.21 = bf16[16,8,32,128]{3,2,1,0:T(8,128)(2,1)S(1)} all-to-all(bf16[16,8,32,128]{3,2,1,0:T(8,128)(2,1)S(1)} %copy.48), channel_id=1, replica_groups=mesh['row'=8,'col'=2,'chan'=16] {'chan'}, dimensions={0} | all-to-all | bytes 2097152 | tf_op jit(solution)/shard_map/all_to_all | solution.py:74
  211.1 0.3 convert_bitcast_fusion
  211.3 1.8 copy.31
  213.1 1.8 reshape.171
  (23 shorter events, 0.1 us)
Async XLA Ops:
  0.0 42.3 %copy-start = (bf16[128,512]{1,0:T(8,128)(2,1)S(1)}, bf16[128,512]{1,0:T(8,128)(2,1)}, u32[]{:S(2)}) copy-start(bf16[128,512]{1,0:T(8,128)(2,1)} %param.13) | copy-start | bytes 393220
  3.5 37.8 %all-to-all-start = ((s16[16,8,32,128]{3,2,1,0:T(8,128)(2,1)}), s16[16,8,32,128]{3,2,1,0:T(8,128)(2,1)S(1)}, u32[]{:S(2)}, u32[]{:S(2)}) async-start(s16[16,8,32,128]{3,2,1,0:T(8,128)(2,1)} %bitcast.1), calls=%async_computation | async-start | bytes 2097152 | tf_op jit(solution)/shard_map/all_to_all | solution.py:27
  16.0 26.3 %copy-start.5 = (f32[128]{0:T(128)S(1)}, f32[128]{0:T(128)}, u32[]{:S(2)}) copy-start(f32[128]{0:T(128)} %param.12) | copy-start | bytes 1540
  16.0 26.3 %copy-start.6 = (f32[128]{0:T(128)S(1)}, f32[128]{0:T(128)}, u32[]{:S(2)}) copy-start(f32[128]{0:T(128)} %param.11) | copy-start | bytes 1540
  52.4 1.6 copy-start.2
  122.7 5.0 %collective-permute-start = (bf16[512,1024]{1,0:T(8,128)(2,1)}, bf16[512,1024]{1,0:T(8,128)(2,1)}, u32[]{:S(2)}, u32[]{:S(2)}) collective-permute-start(bf16[512,1024]{1,0:T(8,128)(2,1)} %squeeze.7), channel_id=1, source_target_pairs={{0,32},{32,0},{64,96},{96,64},{128,160},{160,128},{192,224},{224,1... | collective-permute-start | bytes 3145736 | tf_op jit(solution)/shard_map/ppermute | solution.py:44
  125.1 2.7 %copy-start.1 = (bf16[32,1,16,1024]{3,2,0,1:T(8,128)(2,1)S(1)}, bf16[32,1,16,1024]{3,2,0,1:T(8,128)(2,1)}, u32[]{:S(2)}) copy-start(bf16[32,1,16,1024]{3,2,0,1:T(8,128)(2,1)} %reshape_squeeze.3) | copy-start | bytes 3145732
  129.3 1.2 copy-start.3
  134.6 7.9 %copy-start.4 = (bf16[128,128]{1,0:T(8,128)(2,1)S(1)}, bf16[128,128]{1,0:T(8,128)(2,1)}, u32[]{:S(2)}) copy-start(bf16[128,128]{1,0:T(8,128)(2,1)} %param.17) | copy-start | bytes 98308
  134.6 7.9 %copy-start.7 = (f32[128]{0:T(128)S(1)}, f32[128]{0:T(128)}, u32[]{:S(2)}) copy-start(f32[128]{0:T(128)} %param.15) | copy-start | bytes 1540
  134.6 7.9 %copy-start.8 = (f32[128]{0:T(128)S(1)}, f32[128]{0:T(128)}, u32[]{:S(2)}) copy-start(f32[128]{0:T(128)} %param.16) | copy-start | bytes 1540
  134.6 8.1 %copy-start.9 = (bf16[128,128]{1,0:T(8,128)(2,1)S(1)}, bf16[128,128]{1,0:T(8,128)(2,1)}, u32[]{:S(2)}) copy-start(bf16[128,128]{1,0:T(8,128)(2,1)} %param.14) | copy-start | bytes 98308
  135.9 37.7 %all-to-all-start.2 = ((bf16[256,16,128]{2,1,0:T(8,128)(2,1)}), bf16[256,16,128]{2,1,0:T(8,128)(2,1)S(1)}, u32[]{:S(2)}, u32[]{:S(2)}) async-start(bf16[256,16,128]{2,1,0:T(8,128)(2,1)} %bitcast.79), calls=%async_computation.2 | async-start | bytes 2097152 | tf_op jit(solution)/shard_map/all_to_all | solution.py:51
  174.3 1.6 copy-start.10

commit v2 on v0

v2 whole, which is shorter than its diff:
```python
import jax
import jax.numpy as jnp
from jax import lax
from jax.experimental import pallas as pl
from jax.experimental.pallas import tpu as pltpu
from jax.sharding import PartitionSpec as P

EPS = 1e-05
MESH = pl.DeviceIdType.MESH
STEP = 6.0 / 32767.0
R0, R1, L0, L1 = range(4)


def kernel(
    pair,
    mask,
    norm_gain,
    norm_bias,
    in_weight,
    gate_weight,
    hidden_gain,
    hidden_bias,
    out_weight,
    out,
    enc,
    got,
    flat,
    flat2,
    maskf,
    columns,
    wt,
    pieces,
    sides,
    across,
    rights,
    lefts,
    product,
    plane,
    hidden,
    gate,
    upd,
    owned,
    enc_send,
    enc_recv,
    side_send,
    side_recv,
    plane_send,
    right_recv,
    left_recv,
    twin_send,
    twin_recv,
    prod_send,
    prod_recv,
    hid_send,
    hid_recv,
    upd_send,
    upd_recv,
):
    row, col, chan = lax.axis_index("row"), lax.axis_index("col"), lax.axis_index("chan")
    x, core = row // 2, lax.rem(row, 2)
    y, zhi = chan // 4, lax.rem(chan, 4)
    z = zhi * 2 + col

    def at(r, c, h):
        return {"row": r, "col": c, "chan": h}

    def wait(ref, sem):
        pltpu.make_async_copy(ref, ref, sem).wait()

    def remote(src, dst, send, recv, device):
        pltpu.make_async_remote_copy(
            src_ref=src,
            dst_ref=dst,
            send_sem=send,
            recv_sem=recv,
            device_id=device,
            device_id_type=MESH,
        ).start()

    def block_of(zz):
        return pl.ds(pl.multiple_of((lax.rem(zz, 2) * 4 + zz // 2) * 128, 128), 128)

    barrier = pltpu.get_barrier_semaphore()

    def greet(device):
        pl.semaphore_signal(barrier, inc=1, device_id=device, device_id_type=MESH)

    def greet_chan(t, carry):
        greet(at(row, col, lax.rem(chan + t, 16)))
        return carry

    def greet_z(t, carry):
        greet(at(row, 1 - col, y * 4 + t))
        return carry

    def greet_plane(t, carry):
        greet(at(lax.rem(row + 1 + t // 4, 8), col, lax.rem(t, 4) * 4 + zhi))
        return carry

    lax.fori_loop(1, 16, greet_chan, 0)
    lax.fori_loop(0, 4, greet_z, 0)
    lax.fori_loop(0, 28, greet_plane, 0)

    def encode(q):
        for p in range(16):
            part = pair[:, (p // 4) * 32 + q * 16 :, (p % 4) * 128 :][:, :16, :128]
            enc[q, p] = jnp.round(part * (1.0 / STEP)).astype(jnp.int32).astype(jnp.int16)

    def send_enc(q):
        mine = pl.ds(pl.multiple_of(chan * 8, 8), 8)

        def go(t, carry):
            p = lax.rem(chan + t, 16)
            remote(
                enc.at[q, p], got.at[q, mine], enc_send.at[q], enc_recv.at[q], at(row, col, p)
            )
            return carry

        lax.fori_loop(1, 16, go, 0)
        pltpu.make_async_copy(enc.at[q, chan], got.at[q, mine], enc_recv.at[q]).start()

    encode(0)
    pl.semaphore_wait(barrier, 47)
    send_enc(0)
    encode(1)
    send_enc(1)

    wt[:512] = in_weight[...].astype(jnp.float32).T.astype(jnp.bfloat16)
    wt[512:] = gate_weight[...].astype(jnp.float32).T.astype(jnp.bfloat16)
    columns[0] = jnp.broadcast_to(norm_gain[...], (128, 128)).T
    columns[1] = jnp.broadcast_to(norm_bias[...], (128, 128)).T
    out_t = out_weight[...].astype(jnp.float32).T
    scaled = out_t * hidden_gain[...]
    high = scaled.astype(jnp.bfloat16)
    low = (scaled - high.astype(jnp.float32)).astype(jnp.bfloat16)
    pieces[:, :128] = high
    pieces[:, 128:] = low
    total = jnp.sum(high.astype(jnp.float32) + low.astype(jnp.float32), axis=1, keepdims=True)
    columns[2] = jnp.broadcast_to(total, (128, 128))
    offset = jnp.sum(out_t * hidden_bias[...], axis=1, keepdims=True)
    columns[3] = jnp.broadcast_to(offset, (128, 128))
    rows_mine = pl.ds(pl.multiple_of(y * 32, 32), 32)
    maskf[...] = mask[rows_mine, pl.ds(pl.multiple_of(zhi * 128, 128), 128)].astype(jnp.float32)

    def twice(a):
        return jnp.concatenate([a, a], axis=1)

    def rows_of(ref, i):
        return jnp.concatenate(
            [ref[pl.ds(2 * i, 128, stride=16), :], ref[pl.ds(2 * i + 1, 128, stride=16), :]],
            axis=1,
        )

    def put_rows(ref, i, value):
        ref[pl.ds(2 * i, 128, stride=16), :] = value[:, :128]
        ref[pl.ds(2 * i + 1, 128, stride=16), :] = value[:, 128:]

    def project(q):
        flat[...] = got[q].astype(jnp.int32).astype(jnp.float32).reshape(2048, 128) * STEP

        def step(i, carry):
            value = rows_of(flat, i)
            mean = jnp.sum(value, axis=0, keepdims=True) * (1.0 / 128)
            centred = value - mean
            var = jnp.sum(centred * centred, axis=0, keepdims=True) * (1.0 / 128)
            normed = centred * lax.rsqrt(var + EPS) * twice(columns[0]) + twice(columns[1])
            normed = normed.astype(jnp.bfloat16)
            present = jnp.concatenate(
                [
                    maskf[pl.ds(q * 16 + 2 * i, 1), :],
                    maskf[pl.ds(q * 16 + 2 * i + 1, 1), :],
                ],
                axis=1,
            )

            def proj(k):
                return jnp.dot(
                    wt[k * 128 : k * 128 + 128, :], normed, preferred_element_type=jnp.float32
                )

            put_rows(flat, i, jax.nn.sigmoid(proj(0)) * proj(1) * present)
            put_rows(flat2, i, jax.nn.sigmoid(proj(2)) * proj(3) * present)
            gated = jax.nn.sigmoid(proj(4))
            gate[q, 2 * i] = gated[:, :128]
            gate[q, 2 * i + 1] = gated[:, 128:]
            return carry

        lax.fori_loop(0, 8, step, 0)
        sides[L0 + q] = flat[...].reshape(128, 16, 128).astype(jnp.bfloat16)
        sides[R0 + q] = flat2[...].reshape(128, 16, 128).astype(jnp.bfloat16)

    def send_sides(s):
        def go(t, carry):
            zz = lax.rem(z + t, 8)
            remote(
                sides.at[s, pl.ds(pl.multiple_of(zz * 16, 16), 16)],
                across.at[s, :, :, block_of(z)],
                side_send.at[s],
                side_recv.at[s],
                at(row, lax.rem(zz, 2), y * 4 + zz // 2),
            )
            return carry

        lax.fori_loop(1, 8, go, 0)
        pltpu.make_async_copy(
            sides.at[s, pl.ds(pl.multiple_of(z * 16, 16), 16)],
            across.at[s, :, :, block_of(z)],
            side_recv.at[s],
        ).start()

    def send_plane(s):
        q = s % 2
        ours = pl.ds(pl.multiple_of((row * 4 + y) * 16, 16), 16)
        dst = rights.at[q, ours] if s < L0 else lefts.at[ours]
        recv = right_recv if s < L0 else left_recv
        wait(across.at[s], side_recv.at[s])

        def go(t, carry):
            k = lax.rem(x * 4 + y + t, 16)
            remote(
                across.at[s, k],
                dst,
                plane_send.at[s],
                recv,
                at((k // 4) * 2 + q, col, lax.rem(k, 4) * 4 + zhi),
            )
            return carry

        lax.fori_loop(1, 16, go, 0)

        @pl.when(core == q)
        def _():
            pltpu.make_async_copy(across.at[s, x * 4 + y], dst, recv).start()

        @pl.when(core != q)
        def _():
            go(0, 0)

    wait(got.at[0], enc_recv.at[0])
    project(0)
    send_sides(R0)
    wait(got.at[1], enc_recv.at[1])
    project(1)
    send_sides(R1)
    send_sides(L0)
    send_sides(L1)
    send_plane(R0)
    send_plane(R1)

    wait(rights.at[core], right_recv)
    remote(rights.at[core], rights.at[core], twin_send, twin_recv, at(x * 2 + 1 - core, col, chan))
    send_plane(L0)

    def multiply():
        wait(rights.at[1 - core], twin_recv)
        wait(lefts, left_recv)

        def step(n, carry):
            parts = []
            for m in range(2):
                for yy in range(4):
                    for q in range(2):
                        start = pl.multiple_of((n * 2 + m) * 64 + yy * 16, 16)
                        parts.append(rights[q, pl.ds(start, 16), :])
            block = jnp.concatenate(parts, axis=0)
            result = lax.dot_general(
                lefts[...], block, (((1,), (1,)), ((), ())), preferred_element_type=jnp.float32
            )
            product[:, pl.ds(pl.multiple_of(n * 256, 256), 256)] = result.astype(jnp.bfloat16)
            return carry

        lax.fori_loop(0, 4, step, 0)

        def go(t, carry):
            k = lax.rem(row * 4 + y + t, 32)
            remote(
                product.at[pl.ds(pl.multiple_of(k * 16, 16), 16)],
                plane.at[core, x * 4 + y],
                prod_send,
                prod_recv.at[core],
                at(k // 4, col, lax.rem(k, 4) * 4 + zhi),
            )
            return carry

        lax.fori_loop(1, 32, go, 0)
        pltpu.make_async_copy(
            product.at[pl.ds(pl.multiple_of((row * 4 + y) * 16, 16), 16)],
            plane.at[core, x * 4 + y],
            prod_recv.at[core],
        ).start()

    def send_hidden(q):
        wait(plane.at[q], prod_recv.at[q])
        dst = hidden.at[q, pl.ds(pl.multiple_of(z * 16, 16), 16)]

        def go(t, carry):
            zz = lax.rem(z + t, 8)
            remote(
                plane.at[q, :, :, block_of(zz)],
                dst,
                hid_send.at[q],
                hid_recv.at[q],
                at(row, lax.rem(zz, 2), y * 4 + zz // 2),
            )
            return carry

        lax.fori_loop(1, 8, go, 0)
        pltpu.make_async_copy(plane.at[q, :, :, block_of(z)], dst, hid_recv.at[q]).start()

    @pl.when(core == 0)
    def _():
        multiply()

    send_plane(L1)
    send_hidden(0)

    @pl.when(core == 1)
    def _():
        multiply()

    send_hidden(1)

    def finish(q):
        wait(hidden.at[q], hid_recv.at[q])
        flat[...] = hidden[q].astype(jnp.float32).reshape(2048, 128)

        def step(i, carry):
            value = rows_of(flat, i)
            nu = jnp.sum(value, axis=0, keepdims=True) * (1.0 / 128)
            dev = value - nu
            tau = jnp.sum(dev * dev, axis=0, keepdims=True) * (1.0 / 128)
            short = value.astype(jnp.bfloat16)
            raw = jnp.dot(
                pieces[...],
                jnp.concatenate([short, short], axis=0),
                preferred_element_type=jnp.float32,
            )
            out_rows = (raw - twice(columns[2]) * nu) * lax.rsqrt(tau + EPS) + twice(columns[3])
            gated = jnp.concatenate([gate[q, 2 * i], gate[q, 2 * i + 1]], axis=1)
            put_rows(flat2, i, gated * out_rows)
            return carry

        lax.fori_loop(0, 8, step, 0)
        upd[q] = flat2[...].reshape(128, 16, 128).astype(jnp.bfloat16)
        dst = owned.at[
            :,
            pl.ds(pl.multiple_of(y * 32 + q * 16, 16), 16),
            pl.ds(pl.multiple_of(zhi * 128, 128), 128),
        ]

        def go(t, carry):
            p = lax.rem(chan + t, 16)
            remote(
                upd.at[q, pl.ds(pl.multiple_of(p * 8, 8), 8)],
                dst,
                upd_send.at[q],
                upd_recv,
                at(row, col, p),
            )
            return carry

        lax.fori_loop(1, 16, go, 0)
        pltpu.make_async_copy(
            upd.at[q, pl.ds(pl.multiple_of(chan * 8, 8), 8)], dst, upd_recv
        ).start()

    finish(0)
    finish(1)

    for q in range(2):
        wait(enc.at[q, :15], enc_send.at[q])
        wait(plane.at[q, :14], hid_send.at[q])
        wait(upd.at[q, :120], upd_send.at[q])
    for s in range(4):
        wait(sides.at[s, :112], side_send.at[s])

        @pl.when(core == s % 2)
        def _():
            wait(across.at[s, :15], plane_send.at[s])

        @pl.when(core != s % 2)
        def _():
            wait(across.at[s], plane_send.at[s])

    wait(rights.at[core], twin_send)
    wait(product.at[: 31 * 16], prod_send)
    wait(owned, upd_recv)
    out[...] = owned[...]


def shards(
    pair,
    pair_mask,
    norm_gain,
    norm_bias,
    in_weight,
    gate_weight,
    hidden_gain,
    hidden_bias,
    out_weight,
):
    bf16, f32 = jnp.bfloat16, jnp.float32
    dma = pltpu.SemaphoreType.DMA
    vmem = pl.BlockSpec(memory_space=pltpu.VMEM)
    update = pl.pallas_call(
        kernel,
        out_shape=jax.ShapeDtypeStruct((8, 128, 512), bf16),
        in_specs=[vmem] * 9,
        out_specs=vmem,
        scratch_shapes=[
            pltpu.VMEM((2, 16, 8, 16, 128), jnp.int16),
            pltpu.VMEM((2, 128, 16, 128), jnp.int16),
            pltpu.VMEM((2048, 128), f32),
            pltpu.VMEM((2048, 128), f32),
            pltpu.VMEM((32, 128), f32),
            pltpu.VMEM((4, 128, 128), f32),
            pltpu.VMEM((640, 128), bf16),
            pltpu.VMEM((128, 256), bf16),
            pltpu.VMEM((4, 128, 16, 128), bf16),
            pltpu.VMEM((4, 16, 16, 1024), bf16),
            pltpu.VMEM((2, 512, 1024), bf16),
            pltpu.VMEM((512, 1024), bf16),
            pltpu.VMEM((512, 1024), bf16),
            pltpu.VMEM((2, 16, 16, 1024), bf16),
            pltpu.VMEM((2, 128, 16, 128), bf16),
            pltpu.VMEM((2, 16, 128, 128), f32),
            pltpu.VMEM((2, 128, 16, 128), bf16),
            pltpu.VMEM((8, 128, 512), bf16),
            dma((2,)),
            dma((2,)),
            dma((4,)),
            dma((4,)),
            dma((4,)),
            dma,
            dma,
            dma,
            dma,
            dma,
            dma((2,)),
            dma((2,)),
            dma((2,)),
            dma((2,)),
            dma,
        ],
        compiler_params=pltpu.CompilerParams(
            collective_id=0, has_side_effects=True, vmem_limit_bytes=48 * 2**20
        ),
        name="triangle",
    )(
        pair,
        pair_mask,
        norm_gain.reshape(1, 128),
        norm_bias.reshape(1, 128),
        in_weight,
        gate_weight,
        hidden_gain.reshape(1, 128),
        hidden_bias.reshape(1, 128),
        out_weight,
    )
    return update.astype(f32)


def solution(mesh):
    placed = (P("chan", "row", "col"), P("row", "col"), P(), P(), P(), P(), P(), P(), P())
    return jax.shard_map(
        shards, mesh=mesh, in_specs=placed, out_specs=P("chan", "row", "col"), check_vma=False
    )
```

time: 369 us -> 155 us (0.42)
  the two profiles are of different devices: /device:TPU:35 before, /device:TPU:1 now
where the time goes in v2:
time: 155 us; the launch traced here: 153 us
  Pallas kernels  144 us (93%)
  local copies, waits for them, and re-layouts  7.58 us (5%)
  other arithmetic  1.61 us (1%)
    pallas_call x1, Pallas kernels, shards(): pl.pallas_call(kernel, out_shape=jax.ShapeDtypeStruct((8, 128, 512), bf16...  144 us
    unnamed x18, local copies, waits for them, and re-layouts  7.58 us

profile of v2, /device:TPU:1, one launch (start us, length us, event | category | flops | bytes accessed | tf_op | source)
XLA Modules:
  0.0 153.4 jit_solution(11713775837843583991)
XLA Ops:
  0.0 0.0 copy-start
  0.0 1.6 %copy-done = f32[8,128,512]{2,1,0:T(8,128)S(1)} copy-done((f32[8,128,512]{2,1,0:T(8,128)S(1)}, f32[8,128,512]{2,1,0:T(8,128)}, u32[]{:S(2)}) %copy-start) | copy-done | bytes 2097176
  1.6 0.0 copy-start.1
  1.6 0.9 copy-done.1
  2.5 0.0 copy-start.2
  2.5 0.9 copy-done.2
  3.4 0.0 copy-start.3
  3.4 0.8 copy-done.3
  4.2 0.0 copy-start.4
  4.2 0.8 copy-done.4
  5.0 0.0 copy-start.5
  5.0 0.7 copy-done.5
  5.6 0.0 copy-start.6
  5.6 0.7 copy-done.6
  6.3 0.0 copy-start.7
  6.3 0.7 copy-done.7
  6.9 0.0 copy-start.8
  6.9 0.7 copy-done.8
  7.6 144.2 %triangle.1 = bf16[8,128,512]{2,1,0:T(8,128)(2,1)S(1)} custom-call(f32[8,128,512]{2,1,0:T(8,128)S(1)} %copy-done, s32[128,512]{1,0:T(8,128)S(1)} %copy-done.1, f32[1,128]{1,0:T(1,128)S(1)} %bitcast.4, f32[1,128]{1,0:T(1,128)S(1)} %bitcast.5, bf16[128,512]{1,0:T(8,128)(2,1)S(1)} %copy-done.2, bf16[128,128]{1,0:T(8,128)(2,1)S(1)} %copy-done.3, ...), custom_call_target="tpu_custom_call" | custom-call | tf_op jit(solution)/shard_map/triangle/pallas_call | solution.py:405
  151.8 1.6 %convert_element_type.3 = f32[8,128,512]{2,1,0:T(8,128)} convert(bf16[8,128,512]{2,1,0:T(8,128)(2,1)S(1)} %triangle.1) | non-fusion elementwise | flops 524288 | bytes 3145728 | tf_op jit(solution)/shard_map/convert_element_type | solution.py:460
Async XLA Ops:
  0.0 1.6 %copy-start = (f32[8,128,512]{2,1,0:T(8,128)S(1)}, f32[8,128,512]{2,1,0:T(8,128)}, u32[]{:S(2)}) copy-start(f32[8,128,512]{2,1,0:T(8,128)} %pair.1) | copy-start | bytes 6291460
  1.6 0.9 copy-start.1
  2.5 0.9 copy-start.2
  3.4 0.8 copy-start.3
  4.2 0.8 copy-start.4
  5.0 0.7 copy-start.5
  5.6 0.7 copy-start.6
  6.3 0.7 copy-start.7
  6.9 0.7 copy-start.8

commit v3 on v2

--- a/solution.py
+++ b/solution.py
@@ -12,6 +12,16 @@
 
 
 def kernel(
+    pair_in,
+    mask_in,
+    norm_gain_in,
+    norm_bias_in,
+    in_weight_in,
+    gate_weight_in,
+    hidden_gain_in,
+    hidden_bias_in,
+    out_weight_in,
+    out,
     pair,
     mask,
     norm_gain,
@@ -21,7 +31,6 @@
     hidden_gain,
     hidden_bias,
     out_weight,
-    out,
     enc,
     got,
     flat,
@@ -40,6 +49,8 @@
     gate,
     upd,
     owned,
+    pair_sem,
+    load_sem,
     enc_send,
     enc_recv,
     side_send,
@@ -80,6 +91,30 @@
     def block_of(zz):
         return pl.ds(pl.multiple_of((lax.rem(zz, 2) * 4 + zz // 2) * 128, 128), 128)
 
+    for q in range(2):
+        for k in range(4):
+            pltpu.make_async_copy(
+                pair_in.at[:, k * 32 + q * 16 : k * 32 + q * 16 + 16], pair.at[q, k], pair_sem.at[q]
+            ).start()
+    rows_mine = pl.ds(pl.multiple_of(y * 32, 32), 32)
+    loads = [
+        pltpu.make_async_copy(src, dst, load_sem.at[n])
+        for n, (src, dst) in enumerate(
+            [
+                (mask_in.at[rows_mine, pl.ds(pl.multiple_of(zhi * 128, 128), 128)], mask),
+                (norm_gain_in, norm_gain),
+                (norm_bias_in, norm_bias),
+                (in_weight_in, in_weight),
+                (gate_weight_in, gate_weight),
+                (hidden_gain_in, hidden_gain),
+                (hidden_bias_in, hidden_bias),
+                (out_weight_in, out_weight),
+            ]
+        )
+    ]
+    for load in loads:
+        load.start()
+
     barrier = pltpu.get_barrier_semaphore()
 
     def greet(device):
@@ -102,8 +137,9 @@
     lax.fori_loop(0, 28, greet_plane, 0)
 
     def encode(q):
+        wait(pair.at[q], pair_sem.at[q])
         for p in range(16):
-            part = pair[:, (p // 4) * 32 + q * 16 :, (p % 4) * 128 :][:, :16, :128]
+            part = pair[q, p // 4, :, :, (p % 4) * 128 : (p % 4) * 128 + 128]
             enc[q, p] = jnp.round(part * (1.0 / STEP)).astype(jnp.int32).astype(jnp.int16)
 
     def send_enc(q):
@@ -125,6 +161,8 @@
     encode(1)
     send_enc(1)
 
+    for load in loads:
+        load.wait()
     wt[:512] = in_weight[...].astype(jnp.float32).T.astype(jnp.bfloat16)
     wt[512:] = gate_weight[...].astype(jnp.float32).T.astype(jnp.bfloat16)
     columns[0] = jnp.broadcast_to(norm_gain[...], (128, 128)).T
@@ -139,8 +177,7 @@
     columns[2] = jnp.broadcast_to(total, (128, 128))
     offset = jnp.sum(out_t * hidden_bias[...], axis=1, keepdims=True)
     columns[3] = jnp.broadcast_to(offset, (128, 128))
-    rows_mine = pl.ds(pl.multiple_of(y * 32, 32), 32)
-    maskf[...] = mask[rows_mine, pl.ds(pl.multiple_of(zhi * 128, 128), 128)].astype(jnp.float32)
+    maskf[...] = mask[...].astype(jnp.float32)
 
     def twice(a):
         return jnp.concatenate([a, a], axis=1)
@@ -191,7 +228,7 @@
 
     def send_sides(s):
         def go(t, carry):
-            zz = lax.rem(z + t, 8)
+            zz = lax.rem(z + lax.select(lax.rem(t, 2) == 1, (9 - t) // 2, 4 + t // 2), 8)
             remote(
                 sides.at[s, pl.ds(pl.multiple_of(zz * 16, 16), 16)],
                 across.at[s, :, :, block_of(z)],
@@ -236,15 +273,20 @@
         def _():
             go(0, 0)
 
+    def sent(s):
+        wait(sides.at[s, :112], side_send.at[s])
+
     wait(got.at[0], enc_recv.at[0])
     project(0)
     send_sides(R0)
     wait(got.at[1], enc_recv.at[1])
     project(1)
     send_sides(R1)
+    sent(R0)
     send_sides(L0)
+    send_plane(R0)
+    sent(R1)
     send_sides(L1)
-    send_plane(R0)
     send_plane(R1)
 
     wait(rights.at[core], right_recv)
@@ -294,7 +336,7 @@
         dst = hidden.at[q, pl.ds(pl.multiple_of(z * 16, 16), 16)]
 
         def go(t, carry):
-            zz = lax.rem(z + t, 8)
+            zz = lax.rem(z + lax.select(lax.rem(t, 2) == 1, (9 - t) // 2, 4 + t // 2), 8)
             remote(
                 plane.at[q, :, :, block_of(zz)],
                 dst,
@@ -367,12 +409,15 @@
     finish(0)
     finish(1)
 
+    wait(enc.at[0, :15], enc_send.at[0])
+    wait(enc.at[1, :15], enc_send.at[1])
+    wait(plane.at[0, :14], hid_send.at[0])
+    wait(plane.at[1, :14], hid_send.at[1])
     for q in range(2):
-        wait(enc.at[q, :15], enc_send.at[q])
-        wait(plane.at[q, :14], hid_send.at[q])
         wait(upd.at[q, :120], upd_send.at[q])
+    sent(L0)
+    sent(L1)
     for s in range(4):
-        wait(sides.at[s, :112], side_send.at[s])
 
         @pl.when(core == s % 2)
         def _():
@@ -405,9 +450,18 @@
     update = pl.pallas_call(
         kernel,
         out_shape=jax.ShapeDtypeStruct((8, 128, 512), bf16),
-        in_specs=[vmem] * 9,
+        in_specs=[pl.BlockSpec(memory_space=pltpu.HBM)] * 9,
         out_specs=vmem,
         scratch_shapes=[
+            pltpu.VMEM((2, 4, 8, 16, 512), f32),
+            pltpu.VMEM((32, 128), jnp.int32),
+            pltpu.VMEM((1, 128), f32),
+            pltpu.VMEM((1, 128), f32),
+            pltpu.VMEM((128, 512), bf16),
+            pltpu.VMEM((128, 128), bf16),
+            pltpu.VMEM((1, 128), f32),
+            pltpu.VMEM((1, 128), f32),
+            pltpu.VMEM((128, 128), bf16),
             pltpu.VMEM((2, 16, 8, 16, 128), jnp.int16),
             pltpu.VMEM((2, 128, 16, 128), jnp.int16),
             pltpu.VMEM((2048, 128), f32),
@@ -427,6 +481,8 @@
             pltpu.VMEM((2, 128, 16, 128), bf16),
             pltpu.VMEM((8, 128, 512), bf16),
             dma((2,)),
+            dma((8,)),
+            dma((2,)),
             dma((2,)),
             dma((4,)),
             dma((4,)),
@@ -443,7 +499,7 @@
             dma,
         ],
         compiler_params=pltpu.CompilerParams(
-            collective_id=0, has_side_effects=True, vmem_limit_bytes=48 * 2**20
+            collective_id=0, has_side_effects=True, vmem_limit_bytes=62 * 2**20
         ),
         name="triangle",
     )(

time: 155 us -> 148 us (0.955); the launches traced: 153 us -> 148 us
  local copies, waits for them, and re-layouts: 7.58 us -> 0 us
    unnamed x18 -> x0, local copies, waits for them, and re-layouts: 7.58 us -> none
where the time goes in v3:
time: 148 us
  Pallas kernels  145 us (98%)
  other arithmetic  2.83 us (2%)
    pallas_call x1, Pallas kernels, shards(): pl.pallas_call(kernel, out_shape=jax.ShapeDtypeStruct((8, 128, 512), bf16...  145 us

profile of v3, /device:TPU:1, one launch (start us, length us, event | category | flops | bytes accessed | tf_op | source)
XLA Modules:
  0.0 148.1 jit_solution(12738807991127356229)
XLA Ops:
  0.0 145.3 %triangle.1 = bf16[8,128,512]{2,1,0:T(8,128)(2,1)} custom-call(f32[8,128,512]{2,1,0:T(8,128)} %pair_in.1, s32[128,512]{1,0:T(8,128)} %mask_in.1, f32[1,128]{1,0:T(1,128)} %bitcast.4, f32[1,128]{1,0:T(1,128)} %bitcast.5, bf16[128,512]{1,0:T(8,128)(2,1)} %in_weight_in.1, bf16[128,128]{1,0:T(8,128)(2,1)} %gate_weight_in.1, f32[1,128]{1,0:T(1,128)} %bitcast.6, ...), custom_call_target="tpu_custom_call" | custom-call | tf_op jit(solution)/shard_map/triangle/pallas_call | solution.py:450
  145.3 2.8 %convert_element_type.3 = f32[8,128,512]{2,1,0:T(8,128)} convert(bf16[8,128,512]{2,1,0:T(8,128)(2,1)} %triangle.1) | non-fusion elementwise | flops 524288 | bytes 3145728 | tf_op jit(solution)/shard_map/convert_element_type | solution.py:516

commit v4 on v3

--- a/solution.py
+++ b/solution.py
@@ -147,8 +147,14 @@
 
         def go(t, carry):
             p = lax.rem(chan + t, 16)
+            if q == 1:
+                wait(enc.at[0, 0], enc_send.at[t])
             remote(
-                enc.at[q, p], got.at[q, mine], enc_send.at[q], enc_recv.at[q], at(row, col, p)
+                enc.at[q, p],
+                got.at[q, mine],
+                enc_send.at[t if q == 0 else 0],
+                enc_recv.at[q],
+                at(row, col, p),
             )
             return carry
 
@@ -297,57 +303,71 @@
         wait(rights.at[1 - core], twin_recv)
         wait(lefts, left_recv)
 
-        def step(n, carry):
+        def step(m, carry):
+            n = lax.rem(m + z // 2, 4)
             parts = []
-            for m in range(2):
+            for half in range(2):
                 for yy in range(4):
                     for q in range(2):
-                        start = pl.multiple_of((n * 2 + m) * 64 + yy * 16, 16)
+                        start = pl.multiple_of((n * 2 + half) * 64 + yy * 16, 16)
                         parts.append(rights[q, pl.ds(start, 16), :])
             block = jnp.concatenate(parts, axis=0)
             result = lax.dot_general(
                 lefts[...], block, (((1,), (1,)), ((), ())), preferred_element_type=jnp.float32
             )
-            product[:, pl.ds(pl.multiple_of(n * 256, 256), 256)] = result.astype(jnp.bfloat16)
+            span = pl.ds(pl.multiple_of(n * 256, 256), 256)
+            product[:, span] = result.astype(jnp.bfloat16)
+
+            def go(t, carry):
+                k = lax.rem(row * 4 + y + t, 32)
+                remote(
+                    product.at[pl.ds(pl.multiple_of(k * 16, 16), 16), span],
+                    plane.at[core, x * 4 + y, :, span],
+                    prod_send.at[n],
+                    prod_recv.at[core, n],
+                    at(k // 4, col, lax.rem(k, 4) * 4 + zhi),
+                )
+                return carry
+
+            lax.fori_loop(1, 32, go, 0)
+            pltpu.make_async_copy(
+                product.at[pl.ds(pl.multiple_of((row * 4 + y) * 16, 16), 16), span],
+                plane.at[core, x * 4 + y, :, span],
+                prod_recv.at[core, n],
+            ).start()
             return carry
 
         lax.fori_loop(0, 4, step, 0)
 
-        def go(t, carry):
-            k = lax.rem(row * 4 + y + t, 32)
-            remote(
-                product.at[pl.ds(pl.multiple_of(k * 16, 16), 16)],
-                plane.at[core, x * 4 + y],
-                prod_send,
-                prod_recv.at[core],
-                at(k // 4, col, lax.rem(k, 4) * 4 + zhi),
-            )
-            return carry
-
-        lax.fori_loop(1, 32, go, 0)
-        pltpu.make_async_copy(
-            product.at[pl.ds(pl.multiple_of((row * 4 + y) * 16, 16), 16)],
-            plane.at[core, x * 4 + y],
-            prod_recv.at[core],
-        ).start()
-
     def send_hidden(q):
-        wait(plane.at[q], prod_recv.at[q])
         dst = hidden.at[q, pl.ds(pl.multiple_of(z * 16, 16), 16)]
 
-        def go(t, carry):
-            zz = lax.rem(z + lax.select(lax.rem(t, 2) == 1, (9 - t) // 2, 4 + t // 2), 8)
-            remote(
-                plane.at[q, :, :, block_of(zz)],
-                dst,
-                hid_send.at[q],
-                hid_recv.at[q],
-                at(row, lax.rem(zz, 2), y * 4 + zz // 2),
-            )
-            return carry
-
-        lax.fori_loop(1, 8, go, 0)
-        pltpu.make_async_copy(plane.at[q, :, :, block_of(z)], dst, hid_recv.at[q]).start()
+        def go(m, carry):
+            n = lax.rem(m + z // 2, 4)
+            span = pl.ds(pl.multiple_of(n * 256, 256), 256)
+            wait(plane.at[q, :, :, span], prod_recv.at[q, n])
+            for half in range(2):
+                block = n * 2 + half
+                zz = lax.rem(block, 4) * 2 + block // 4
+                src = plane.at[q, :, :, pl.ds(pl.multiple_of(block * 128, 128), 128)]
+
+                @pl.when(zz == z)
+                def _():
+                    pltpu.make_async_copy(src, dst, hid_recv.at[q]).start()
+
+                @pl.when(zz != z)
+                def _():
+                    remote(
+                        src,
+                        dst,
+                        hid_send.at[q],
+                        hid_recv.at[q],
+                        at(row, lax.rem(zz, 2), y * 4 + zz // 2),
+                    )
+
+            return carry
+
+        lax.fori_loop(0, 4, go, 0)
 
     @pl.when(core == 0)
     def _():
@@ -409,8 +429,7 @@
     finish(0)
     finish(1)
 
-    wait(enc.at[0, :15], enc_send.at[0])
-    wait(enc.at[1, :15], enc_send.at[1])
+    wait(enc.at[1, :15], enc_send.at[0])
     wait(plane.at[0, :14], hid_send.at[0])
     wait(plane.at[1, :14], hid_send.at[1])
     for q in range(2):
@@ -428,7 +447,8 @@
             wait(across.at[s], plane_send.at[s])
 
     wait(rights.at[core], twin_send)
-    wait(product.at[: 31 * 16], prod_send)
+    for n in range(4):
+        wait(product.at[:496, :256], prod_send.at[n])
     wait(owned, upd_recv)
     out[...] = owned[...]
 
@@ -482,7 +502,7 @@
             pltpu.VMEM((8, 128, 512), bf16),
             dma((2,)),
             dma((8,)),
-            dma((2,)),
+            dma((16,)),
             dma((2,)),
             dma((4,)),
             dma((4,)),
@@ -491,8 +511,8 @@
             dma,
             dma,
             dma,
-            dma,
-            dma((2,)),
+            dma((4,)),
+            dma((2, 4)),
             dma((2,)),
             dma((2,)),
             dma((2,)),

time: 148 us -> 145 us (0.980)
  Pallas kernels: 145 us -> 142 us
    pallas_call x1, Pallas kernels: 145 us -> 142 us  [shards(): pl.pallas_call(kernel, out_shape=jax.ShapeDtypeStruct((8, 128, 512), bf16...]
where the time goes in v4:
time: 145 us; the launch traced here: 144 us
  Pallas kernels  142 us (98%)
  other arithmetic  2.83 us (2%)
    pallas_call x1, Pallas kernels, shards(): pl.pallas_call(kernel, out_shape=jax.ShapeDtypeStruct((8, 128, 512), bf16...  142 us

profile of v4, /device:TPU:1, one launch (start us, length us, event | category | flops | bytes accessed | tf_op | source)
XLA Modules:
  0.0 144.5 jit_solution(8204114525787290400)
XLA Ops:
  0.0 141.6 %triangle.1 = bf16[8,128,512]{2,1,0:T(8,128)(2,1)} custom-call(f32[8,128,512]{2,1,0:T(8,128)} %pair_in.1, s32[128,512]{1,0:T(8,128)} %mask_in.1, f32[1,128]{1,0:T(1,128)} %bitcast.4, f32[1,128]{1,0:T(1,128)} %bitcast.5, bf16[128,512]{1,0:T(8,128)(2,1)} %in_weight_in.1, bf16[128,128]{1,0:T(8,128)(2,1)} %gate_weight_in.1, f32[1,128]{1,0:T(1,128)} %bitcast.6, ...), custom_call_target="tpu_custom_call" | custom-call | tf_op jit(solution)/shard_map/triangle/pallas_call | solution.py:470
  141.7 2.8 %convert_element_type.3 = f32[8,128,512]{2,1,0:T(8,128)} convert(bf16[8,128,512]{2,1,0:T(8,128)(2,1)} %triangle.1) | non-fusion elementwise | flops 524288 | bytes 3145728 | tf_op jit(solution)/shard_map/convert_element_type | solution.py:536

commit v5 on v4

--- a/solution.py
+++ b/solution.py
@@ -232,72 +232,84 @@
         sides[L0 + q] = flat[...].reshape(128, 16, 128).astype(jnp.bfloat16)
         sides[R0 + q] = flat2[...].reshape(128, 16, 128).astype(jnp.bfloat16)
 
-    def send_sides(s):
+    def send_sides(s, g):
+        mine = pl.ds(g * 8, 8)
+
         def go(t, carry):
             zz = lax.rem(z + lax.select(lax.rem(t, 2) == 1, (9 - t) // 2, 4 + t // 2), 8)
             remote(
-                sides.at[s, pl.ds(pl.multiple_of(zz * 16, 16), 16)],
-                across.at[s, :, :, block_of(z)],
-                side_send.at[s],
-                side_recv.at[s],
+                sides.at[s, pl.ds(pl.multiple_of(zz * 16 + g * 8, 8), 8)],
+                across.at[s, mine, :, block_of(z)],
+                side_send.at[s, g],
+                side_recv.at[s, g],
                 at(row, lax.rem(zz, 2), y * 4 + zz // 2),
             )
             return carry
 
         lax.fori_loop(1, 8, go, 0)
         pltpu.make_async_copy(
-            sides.at[s, pl.ds(pl.multiple_of(z * 16, 16), 16)],
-            across.at[s, :, :, block_of(z)],
-            side_recv.at[s],
+            sides.at[s, pl.ds(pl.multiple_of(z * 16 + g * 8, 8), 8)],
+            across.at[s, mine, :, block_of(z)],
+            side_recv.at[s, g],
         ).start()
 
-    def send_plane(s):
+    def sent(s, g):
+        wait(sides.at[s, :56], side_send.at[s, g])
+
+    def send_plane(s, g):
         q = s % 2
         ours = pl.ds(pl.multiple_of((row * 4 + y) * 16, 16), 16)
         dst = rights.at[q, ours] if s < L0 else lefts.at[ours]
         recv = right_recv if s < L0 else left_recv
-        wait(across.at[s], side_recv.at[s])
+        wait(across.at[s, g * 8 : g * 8 + 8], side_recv.at[s, g])
 
         def go(t, carry):
-            k = lax.rem(x * 4 + y + t, 16)
+            k = lax.rem(x * 2 + y // 2 + t, 8)
             remote(
-                across.at[s, k],
+                across.at[s, g * 8 + k],
                 dst,
                 plane_send.at[s],
                 recv,
-                at((k // 4) * 2 + q, col, lax.rem(k, 4) * 4 + zhi),
-            )
-            return carry
-
-        lax.fori_loop(1, 16, go, 0)
-
-        @pl.when(core == q)
+                at((k // 2) * 2 + q, col, (lax.rem(k, 2) * 2 + g) * 4 + zhi),
+            )
+            return carry
+
+        lax.fori_loop(1, 8, go, 0)
+        here = jnp.logical_and(core == q, lax.rem(y, 2) == g)
+
+        @pl.when(here)
         def _():
-            pltpu.make_async_copy(across.at[s, x * 4 + y], dst, recv).start()
-
-        @pl.when(core != q)
+            pltpu.make_async_copy(across.at[s, g * 8 + x * 2 + y // 2], dst, recv).start()
+
+        @pl.when(jnp.logical_not(here))
         def _():
             go(0, 0)
 
-    def sent(s):
-        wait(sides.at[s, :112], side_send.at[s])
-
     wait(got.at[0], enc_recv.at[0])
     project(0)
-    send_sides(R0)
+    send_sides(R0, 0)
+    send_sides(R0, 1)
     wait(got.at[1], enc_recv.at[1])
     project(1)
-    send_sides(R1)
-    sent(R0)
-    send_sides(L0)
-    send_plane(R0)
-    sent(R1)
-    send_sides(L1)
-    send_plane(R1)
+    send_sides(R1, 0)
+    send_sides(R1, 1)
+    for g in range(2):
+        sent(R0, g)
+        send_sides(L0, g)
+        send_plane(R0, g)
+    sent(R1, 0)
+    sent(R1, 1)
+    send_plane(R1, 0)
+    send_plane(R1, 1)
+    for g in range(2):
+        sent(L0, g)
+        send_sides(L1, g)
 
     wait(rights.at[core], right_recv)
     remote(rights.at[core], rights.at[core], twin_send, twin_recv, at(x * 2 + 1 - core, col, chan))
-    send_plane(L0)
+    send_plane(L0, 0)
+    send_plane(L0, 1)
+    place = lax.rem(y, 2) * 8 + x * 2 + y // 2
 
     def multiply():
         wait(rights.at[1 - core], twin_recv)
@@ -322,9 +334,9 @@
                 k = lax.rem(row * 4 + y + t, 32)
                 remote(
                     product.at[pl.ds(pl.multiple_of(k * 16, 16), 16), span],
-                    plane.at[core, x * 4 + y, :, span],
+                    plane.at[core, place, :, span],
                     prod_send.at[n],
-                    prod_recv.at[core, n],
+                    prod_recv.at[core * 2 + lax.rem(y, 2), n],
                     at(k // 4, col, lax.rem(k, 4) * 4 + zhi),
                 )
                 return carry
@@ -332,24 +344,25 @@
             lax.fori_loop(1, 32, go, 0)
             pltpu.make_async_copy(
                 product.at[pl.ds(pl.multiple_of((row * 4 + y) * 16, 16), 16), span],
-                plane.at[core, x * 4 + y, :, span],
-                prod_recv.at[core, n],
+                plane.at[core, place, :, span],
+                prod_recv.at[core * 2 + lax.rem(y, 2), n],
             ).start()
             return carry
 
         lax.fori_loop(0, 4, step, 0)
 
-    def send_hidden(q):
-        dst = hidden.at[q, pl.ds(pl.multiple_of(z * 16, 16), 16)]
+    def send_hidden(q, g):
+        part = pl.ds(g * 8, 8)
+        dst = hidden.at[q, pl.ds(pl.multiple_of(z * 16 + g * 8, 8), 8)]
 
         def go(m, carry):
             n = lax.rem(m + z // 2, 4)
             span = pl.ds(pl.multiple_of(n * 256, 256), 256)
-            wait(plane.at[q, :, :, span], prod_recv.at[q, n])
+            wait(plane.at[q, part, :, span], prod_recv.at[q * 2 + g, n])
             for half in range(2):
                 block = n * 2 + half
                 zz = lax.rem(block, 4) * 2 + block // 4
-                src = plane.at[q, :, :, pl.ds(pl.multiple_of(block * 128, 128), 128)]
+                src = plane.at[q, part, :, pl.ds(pl.multiple_of(block * 128, 128), 128)]
 
                 @pl.when(zz == z)
                 def _():
@@ -373,14 +386,17 @@
     def _():
         multiply()
 
-    send_plane(L1)
-    send_hidden(0)
+    send_plane(L1, 0)
+    send_hidden(0, 0)
+    send_plane(L1, 1)
+    send_hidden(0, 1)
 
     @pl.when(core == 1)
     def _():
         multiply()
 
-    send_hidden(1)
+    send_hidden(1, 0)
+    send_hidden(1, 1)
 
     def finish(q):
         wait(hidden.at[q], hid_recv.at[q])
@@ -434,8 +450,8 @@
     wait(plane.at[1, :14], hid_send.at[1])
     for q in range(2):
         wait(upd.at[q, :120], upd_send.at[q])
-    sent(L0)
-    sent(L1)
+    for g in range(2):
+        sent(L1, g)
     for s in range(4):
 
         @pl.when(core == s % 2)
@@ -504,15 +520,15 @@
             dma((8,)),
             dma((16,)),
             dma((2,)),
-            dma((4,)),
-            dma((4,)),
+            dma((4, 2)),
+            dma((4, 2)),
             dma((4,)),
             dma,
             dma,
             dma,
             dma,
             dma((4,)),
-            dma((2, 4)),
+            dma((4, 4)),
             dma((2,)),
             dma((2,)),
             dma((2,)),

time: 145 us -> 141 us (0.972)
  Pallas kernels: 142 us -> 138 us
    pallas_call x1, Pallas kernels: 142 us -> 138 us  [shards(): pl.pallas_call(kernel, out_shape=jax.ShapeDtypeStruct((8, 128, 512), bf16...]
where the time goes in v5:
time: 141 us
  Pallas kernels  138 us (98%)
  other arithmetic  2.83 us (2%)
    pallas_call x1, Pallas kernels, shards(): pl.pallas_call(kernel, out_shape=jax.ShapeDtypeStruct((8, 128, 512), bf16...  138 us
    convert_element_type x1, other arithmetic, shards(): return update.astype(f32)  2.83 us

profile of v5, /device:TPU:1, one launch (start us, length us, event | category | flops | bytes accessed | tf_op | source)
XLA Modules:
  0.0 141.1 jit_solution(10028141995224797029)
XLA Ops:
  0.0 138.2 %triangle.1 = bf16[8,128,512]{2,1,0:T(8,128)(2,1)} custom-call(f32[8,128,512]{2,1,0:T(8,128)} %pair_in.1, s32[128,512]{1,0:T(8,128)} %mask_in.1, f32[1,128]{1,0:T(1,128)} %bitcast.4, f32[1,128]{1,0:T(1,128)} %bitcast.5, bf16[128,512]{1,0:T(8,128)(2,1)} %in_weight_in.1, bf16[128,128]{1,0:T(8,128)(2,1)} %gate_weight_in.1, f32[1,128]{1,0:T(1,128)} %bitcast.6, ...), custom_call_target="tpu_custom_call" | custom-call | tf_op jit(solution)/shard_map/triangle/pallas_call | solution.py:486
  138.2 2.8 %convert_element_type.3 = f32[8,128,512]{2,1,0:T(8,128)} convert(bf16[8,128,512]{2,1,0:T(8,128)(2,1)} %triangle.1) | non-fusion elementwise | flops 524288 | bytes 3145728 | tf_op jit(solution)/shard_map/convert_element_type | solution.py:552

commit v6 on v5

--- a/solution.py
+++ b/solution.py
@@ -467,6 +467,10 @@
         wait(product.at[:496, :256], prod_send.at[n])
     wait(owned, upd_recv)
     out[...] = owned[...]
+
+
+def widen(narrow, wide):
+    wide[...] = narrow[...].astype(jnp.float32)
 
 
 def shards(
@@ -549,7 +553,15 @@
         hidden_bias.reshape(1, 128),
         out_weight,
     )
-    return update.astype(f32)
+    block = pl.BlockSpec((4, 128, 512), lambda n: (n, 0, 0))
+    return pl.pallas_call(
+        widen,
+        grid=(2,),
+        out_shape=jax.ShapeDtypeStruct((8, 128, 512), f32),
+        in_specs=[block],
+        out_specs=block,
+        name="widen",
+    )(update)
 
 
 def solution(mesh):

time: 141 us -> 141 us (level)
  Pallas kernels: 138 us -> 141 us
  other arithmetic: 2.83 us -> 0 us
    convert_element_type x1 -> x0, other arithmetic: 2.83 us -> none  [shards(): return update.astype(f32)]
    pallas_call x0 -> x1, Pallas kernels: none -> 2.44 us  [shards(): pl.pallas_call(widen, grid=(2,), out_shape=jax.ShapeDtypeStruct((8, 128,...]
where the time goes in v6:
time: 141 us
  Pallas kernels  141 us (100%)
    pallas_call x1, Pallas kernels, shards(): pl.pallas_call(kernel, out_shape=jax.ShapeDtypeStruct((8, 128, 512), bf16...  138 us

profile of v6, /device:TPU:1, one launch (start us, length us, event | category | flops | bytes accessed | tf_op | source)
XLA Modules:
  0.0 140.7 jit_solution(14421378446343636378)
XLA Ops:
  0.0 138.2 %triangle.1.narrow = bf16[8,128,512]{2,1,0:T(8,128)(2,1)} custom-call(f32[8,128,512]{2,1,0:T(8,128)} %pair_in.1, s32[128,512]{1,0:T(8,128)} %mask_in.1, f32[1,128]{1,0:T(1,128)} %bitcast.4, f32[1,128]{1,0:T(1,128)} %bitcast.5, bf16[128,512]{1,0:T(8,128)(2,1)} %in_weight_in.1, bf16[128,128]{1,0:T(8,128)(2,1)} %gate_weight_in.1, f32[1,128]{1,0:T(1,128)} %bitcast.6, ...), custom_call_target="tpu_custom_call" | custom-call | tf_op jit(solution)/shard_map/triangle/pallas_call | solution.py:490
  138.2 2.4 %widen.1 = f32[8,128,512]{2,1,0:T(8,128)} custom-call(bf16[8,128,512]{2,1,0:T(8,128)(2,1)} %triangle.1.narrow), custom_call_target="tpu_custom_call" | custom-call | tf_op jit(solution)/shard_map/widen/pallas_call | solution.py:557
